TPU v7x, 32 devices: a whole 2x2x4 slice. The times are simulated.
32 devices in a mesh: seq: 8 (over z, y), head: 4 (over x, core).
Axes of the slice: x: 2, y: 2, z: 4, core: 2. Of those that a mesh axis runs over, the one named last changes fastest.
Arguments:
- layer_input: bfloat16 [4, 1024, 8192], P('head', 'seq'), may hold values from -6 to 6
- out_grad: bfloat16 [4, 1024, 8192], P('head', 'seq'), may hold values from -6 to 6
- attention_out: bfloat16 [4, 1024, 4096], P('head', 'seq'), may hold values from -6 to 6
- frozen_output_grad: bfloat16 [4, 1024, 4096], P('head', 'seq'), may hold values from -6 to 6
- query_rows: bfloat16 [4, 1024, 4096], P('head', 'seq'), may hold values from -120 to 120
- key_rows: bfloat16 [4, 1024, 512], P('head', 'seq'), may hold values from -4 to 4
- value_rows: bfloat16 [4, 1024, 512], P('head', 'seq'), may hold values from -6 to 6
- seg_lengths: int32 [4, 8], P('head'), may hold values from 1 to 256, 1024 in all within a row
- use_list: int32 [4, 8], replicated, may hold values from 0 to 31, as said below
- store_map: int32 [32], replicated, may hold values from 0 to 31, as said below
- query_down: float32 [32, 64, 8192], P('head', None, 'seq'), may hold values from -0.0625 to 0.0625
- query_up: float32 [32, 64, 4096], P('head', None, 'seq'), may hold values from -0.75 to 0.75
- output_down: float32 [32, 64, 4096], P('head', None, 'seq'), may hold values from -0.09375 to 0.09375
- output_up: float32 [32, 64, 8192], P('head', None, 'seq'), may hold values from -0.75 to 0.75
Outputs:
- grad_query_down: float32 [32, 64, 8192], P('head', None, 'seq')
- grad_query_up: float32 [32, 64, 4096], P('head', None, 'seq')
- grad_output_down: float32 [32, 64, 4096], P('head', None, 'seq')
- grad_output_up: float32 [32, 64, 8192], P('head', None, 'seq')
Inputs may be any that keep to these rules, and one draw needn't show every extreme that they name: `use_list`: each row names 8 distinct tenants. Counting a tenant's store index as store_map[tenant] // 8, a row names at most 2 tenants of one store index, and exactly 2 of some store index in every row. A permutation: tenant t's adapters are in slot store_map[t]. `seg_lengths`: each row sums to 1024.
All inputs are finite; a program needn't handle non-finite values.
Results may differ from a plain program's by a relative error of at most 0.024.
Values may be sent and summed in bfloat16 or wider, within the bound.
A program may use at most 128 MiB of HBM per device.

v0:
```python
import math
import jax
import jax.numpy as jnp
from jax import lax
from jax.sharding import PartitionSpec as P

QH = 32
KVH = 4
HD = 128
CAP = 2
adapter_scale = 2.0
big_negative = -1e30
highest = lax.Precision.HIGHEST


def contract_axes(left_side, right_side, left_dim, right_dim):
    return lax.dot_general(
        left_side,
        right_side,
        (((left_dim,), (right_dim,)), ((), ())),
        preferred_element_type=jnp.float32,
    )


def narrow(full_rows, tenant_row_mask, rank_size):
    length, used_count = tenant_row_mask.shape
    return jnp.sum(
        full_rows.reshape(length, used_count, rank_size) * tenant_row_mask[:, :, None], axis=1
    )


def widened_rows(low_rows, tenant_row_mask):
    length, used_count = tenant_row_mask.shape
    spread_rows = tenant_row_mask.astype(jnp.bfloat16)[:, :, None] * low_rows[:, None, :]
    return spread_rows.reshape(length, used_count * low_rows.shape[1])


def request_tables(use_list, store_map, slots_dev):
    tenants = store_map.shape[0]
    used_count = use_list.shape[1]
    matches = use_list[:, :, None] == jnp.arange(tenants, dtype=jnp.int32)[None, None, :]
    slot_index = jnp.sum(jnp.where(matches, store_map[None, None, :], 0), axis=2)
    owner_index = slot_index // slots_dev
    local_slot = slot_index % slots_dev
    same_owner = (owner_index[:, :, None] == owner_index[:, None, :]).astype(jnp.int32)
    indices = jnp.arange(used_count, dtype=jnp.int32)
    earlier = (indices[None, :] < indices[:, None]).astype(jnp.int32)
    rank_index = jnp.sum(same_owner * earlier[None, :, :], axis=2)
    return (owner_index, local_slot, rank_index)


def attention_grad(query_heads, key_heads, value_heads, gradient_heads, segment, key_span):
    length, head_count, head_width = query_heads.shape
    block_rows = min(512, length)
    window = block_rows + key_span
    factor = 1.0 / math.sqrt(head_width)
    padded_keys = jnp.pad(key_heads, ((key_span, 0), (0, 0), (0, 0)))
    padded_values = jnp.pad(value_heads, ((key_span, 0), (0, 0), (0, 0)))
    padded_segment = jnp.concatenate([jnp.full((key_span,), -1, jnp.int32), segment])

    def one_block(row_start):
        query_block = lax.dynamic_slice_in_dim(query_heads, row_start, block_rows, 0)
        grad_block = lax.dynamic_slice_in_dim(gradient_heads, row_start, block_rows, 0)
        key_block = lax.dynamic_slice_in_dim(padded_keys, row_start, window, 0)
        value_block = lax.dynamic_slice_in_dim(padded_values, row_start, window, 0)
        query_segment = lax.dynamic_slice_in_dim(segment, row_start, block_rows, 0)
        key_segment = lax.dynamic_slice_in_dim(padded_segment, row_start, window, 0)
        query_pos = row_start + jnp.arange(block_rows, dtype=jnp.int32)
        key_pos = row_start - key_span + jnp.arange(window, dtype=jnp.int32)
        allowed = (query_segment[:, None] == key_segment[None, :]) & (
            key_pos[None, :] <= query_pos[:, None]
        )
        scores = (
            jnp.einsum("qhd,khd->hqk", query_block, key_block, preferred_element_type=jnp.float32)
            * factor
        )
        scores = jnp.where(allowed[None, :, :], scores, big_negative)
        row_max = jnp.max(scores, axis=2, keepdims=True)
        weights = jnp.exp(scores - row_max)
        probabilities = weights / jnp.sum(weights, axis=2, keepdims=True)
        prob_grad = jnp.einsum(
            "qhd,khd->hqk", grad_block, value_block, preferred_element_type=jnp.float32
        )
        inner = jnp.sum(probabilities * prob_grad, axis=2, keepdims=True)
        score_grad = (probabilities * (prob_grad - inner)).astype(jnp.bfloat16)
        query_gradient = (
            jnp.einsum("hqk,khd->qhd", score_grad, key_block, preferred_element_type=jnp.float32)
            * factor
        )
        return query_gradient.astype(jnp.bfloat16)

    starts = jnp.arange(0, length, block_rows, dtype=jnp.int32)
    return lax.map(one_block, starts).reshape(length, head_count * head_width)


def shards(
    layer_input,
    out_grad,
    attention_out,
    frozen_output_grad,
    query_rows,
    key_rows,
    value_rows,
    seg_lengths,
    use_list,
    store_map,
    query_down,
    query_up,
    output_down,
    output_up,
):
    slots_dev = query_down.shape[0]
    rank_size = query_down.shape[1]
    group_size = QH // KVH
    input_columns, gradient_columns, head_outputs, base_heads, query_heads = (
        lax.all_to_all(layer_input[0], "seq", split_axis=1, concat_axis=0, tiled=True),
        lax.all_to_all(out_grad[0], "seq", split_axis=1, concat_axis=0, tiled=True),
        lax.all_to_all(attention_out[0], "seq", split_axis=1, concat_axis=0, tiled=True),
        lax.all_to_all(frozen_output_grad[0], "seq", split_axis=1, concat_axis=0, tiled=True),
        lax.all_to_all(query_rows[0], "seq", split_axis=1, concat_axis=0, tiled=True),
    )
    length = input_columns.shape[0]
    heads_here = query_heads.shape[1] // HD
    first_head = lax.axis_index("seq") * heads_here
    gathered_keys, gathered_values = (
        lax.all_gather(key_rows[0], "seq", axis=0, tiled=True),
        lax.all_gather(value_rows[0], "seq", axis=0, tiled=True),
    )
    kv_index = (first_head + jnp.arange(heads_here, dtype=jnp.int32)) // group_size
    key_heads = jnp.take(gathered_keys.reshape(length, KVH, HD), kv_index, axis=1)
    value_heads = jnp.take(gathered_values.reshape(length, KVH, HD), kv_index, axis=1)
    owner_index, local_slot, rank_index = request_tables(use_list, store_map, slots_dev)
    my_index = lax.axis_index("head")
    batch_count = use_list.shape[0]
    cap_ids = jnp.arange(CAP, dtype=jnp.int32)
    slot_ids = jnp.arange(slots_dev, dtype=jnp.int32)
    matched = (
        (owner_index == my_index)[:, :, None, None]
        & (rank_index[:, :, None, None] == cap_ids[None, None, :, None])
        & (local_slot[:, :, None, None] == slot_ids[None, None, None, :])
    )
    select = jnp.sum(matched.astype(jnp.float32), axis=1)

    def pack_slots(store_part):
        return jnp.einsum("mcl,lrw->mcrw", select, store_part, precision=highest).astype(
            jnp.bfloat16
        )

    fetched = (
        lax.all_to_all(pack_slots(query_down), "head", split_axis=0, concat_axis=0, tiled=True),
        lax.all_to_all(pack_slots(query_up), "head", split_axis=0, concat_axis=0, tiled=True),
        lax.all_to_all(pack_slots(output_down), "head", split_axis=0, concat_axis=0, tiled=True),
        lax.all_to_all(pack_slots(output_up), "head", split_axis=0, concat_axis=0, tiled=True),
    )
    mine_owner = lax.dynamic_index_in_dim(owner_index, my_index, 0, keepdims=False)
    mine_rank = lax.dynamic_index_in_dim(rank_index, my_index, 0, keepdims=False)
    store_ids = jnp.arange(batch_count, dtype=jnp.int32)
    picker = (
        (mine_owner[:, None, None] == store_ids[None, :, None])
        & (mine_rank[:, None, None] == cap_ids[None, None, :])
    ).astype(jnp.float32)
    picker_half = picker.astype(jnp.bfloat16)

    def unpack(received):
        chosen = jnp.einsum(
            "ijc,jcrw->irw", picker_half, received, preferred_element_type=jnp.float32
        ).astype(jnp.bfloat16)
        return chosen.reshape(chosen.shape[0] * chosen.shape[1], chosen.shape[2])

    flattened_list = [unpack(received) for received in fetched]
    lengths = seg_lengths[0]
    used_count = lengths.shape[0]
    offsets = jnp.cumsum(lengths) - lengths
    positions = jnp.arange(length, dtype=jnp.int32)
    segment = jnp.sum((positions[:, None] >= offsets[None, :]).astype(jnp.int32), axis=1) - 1
    tenant_row_mask = (segment[:, None] == jnp.arange(used_count, dtype=jnp.int32)[None, :]).astype(
        jnp.float32
    )
    partial_out = narrow(
        contract_axes(head_outputs, flattened_list[2], 1, 1), tenant_row_mask, rank_size
    )
    partial_grad = narrow(
        contract_axes(gradient_columns, flattened_list[3], 1, 1), tenant_row_mask, rank_size
    )
    partial_query = narrow(
        contract_axes(input_columns, flattened_list[0], 1, 1), tenant_row_mask, rank_size
    )
    summed_out, summed_grad, summed_query = (
        lax.psum(partial_out.astype(jnp.bfloat16), "seq").astype(jnp.float32),
        lax.psum(partial_grad.astype(jnp.bfloat16), "seq").astype(jnp.float32),
        lax.psum(partial_query.astype(jnp.bfloat16), "seq").astype(jnp.float32),
    )
    low_rank_output = summed_out.astype(jnp.bfloat16)
    low_grad = summed_grad.astype(jnp.bfloat16)
    low_rank_query = summed_query.astype(jnp.bfloat16)
    widened_gradient = widened_rows(low_grad, tenant_row_mask)
    gradient_heads = (
        base_heads.astype(jnp.float32)
        + adapter_scale
        * jnp.dot(widened_gradient, flattened_list[2], preferred_element_type=jnp.float32)
    ).astype(jnp.bfloat16)
    query_gradient = attention_grad(
        query_heads.reshape(length, heads_here, HD),
        key_heads,
        value_heads,
        gradient_heads.reshape(length, heads_here, HD),
        segment,
        length // 4,
    )
    partial_back = narrow(
        contract_axes(query_gradient, flattened_list[1], 1, 1), tenant_row_mask, rank_size
    )
    low_rank_back = lax.psum(partial_back.astype(jnp.bfloat16), "seq")
    outer_products = (
        adapter_scale
        * contract_axes(widened_rows(low_rank_back, tenant_row_mask), input_columns, 0, 0),
        adapter_scale
        * contract_axes(widened_rows(low_rank_query, tenant_row_mask), query_gradient, 0, 0),
        adapter_scale * contract_axes(widened_gradient, head_outputs, 0, 0),
        adapter_scale
        * contract_axes(widened_rows(low_rank_output, tenant_row_mask), gradient_columns, 0, 0),
    )

    def spread(gradient):
        pieces = gradient.reshape(used_count, rank_size, gradient.shape[1])
        return jnp.einsum("ijc,irw->jcrw", picker, pieces, precision=highest)

    returned = (
        lax.all_to_all(
            spread(outer_products[0]).astype(jnp.bfloat16),
            "head",
            split_axis=0,
            concat_axis=0,
            tiled=True,
        ).astype(jnp.float32),
        lax.all_to_all(
            spread(outer_products[1]).astype(jnp.bfloat16),
            "head",
            split_axis=0,
            concat_axis=0,
            tiled=True,
        ).astype(jnp.float32),
        lax.all_to_all(
            spread(outer_products[2]).astype(jnp.bfloat16),
            "head",
            split_axis=0,
            concat_axis=0,
            tiled=True,
        ).astype(jnp.float32),
        lax.all_to_all(
            spread(outer_products[3]).astype(jnp.bfloat16),
            "head",
            split_axis=0,
            concat_axis=0,
            tiled=True,
        ).astype(jnp.float32),
    )

    def settle(received):
        return jnp.einsum("mcl,mcrw->lrw", select, received, precision=highest)

    return (settle(returned[0]), settle(returned[1]), settle(returned[2]), settle(returned[3]))


def solution(mesh):
    placed = (
        P("head", "seq", None),
        P("head", "seq", None),
        P("head", "seq", None),
        P("head", "seq", None),
        P("head", "seq", None),
        P("head", "seq", None),
        P("head", "seq", None),
        P("head", None),
        P(),
        P(),
        P("head", None, "seq"),
        P("head", None, "seq"),
        P("head", None, "seq"),
        P("head", None, "seq"),
    )
    return jax.shard_map(
        shards,
        mesh=mesh,
        in_specs=placed,
        out_specs=(
            P("head", None, "seq"),
            P("head", None, "seq"),
            P("head", None, "seq"),
            P("head", None, "seq"),
        ),
        check_vma=False,
    )
```

profile of v0, /device:TPU:0, one launch (start us, length us, event | category | flops | bytes accessed | tf_op | source)
XLA Modules:
  0.0 579.0 jit_solution(9823844953946376288)
XLA Ops:
  8.7 3.1 convolution_convert_fusion.1
  13.1 4.2 all-to-all-start.4
  20.1 6.7 %all-to-all-done.4 = bf16[4,2,64,512]{3,1,2,0:T(2,128)(2,1)} async-done(((bf16[4,2,64,512]{3,1,2,0:T(2,128)(2,1)}), bf16[4,2,64,512]{3,1,2,0:T(2,128)(2,1)}, u32[]{:S(2)}, u32[]{:S(2)}) %all-to-all-start.4) | async-done | bytes 524320 | tf_op jit(solution)/shard_map/all_to_all | solution.py:152
  26.7 3.5 all-to-all-start.5
  30.2 3.8 fusion.31
  35.8 3.2 all-to-all-done.5
  39.8 3.7 all-to-all-start.2
  43.5 5.4 fusion.34
  50.7 7.2 %all-to-all-done.2 = bf16[4,2,64,1024]{3,1,2,0:T(2,128)(2,1)S(1)} async-done(((bf16[4,2,64,1024]{3,1,2,0:T(2,128)(2,1)}), bf16[4,2,64,1024]{3,1,2,0:T(2,128)(2,1)S(1)}, u32[]{:S(2)}, u32[]{:S(2)}) %all-to-all-start.2) | async-done | bytes 1048608 | tf_op jit(solution)/shard_map/all_to_all | solution.py:153
  58.9 3.5 all-to-all-start.8
  63.8 13.1 %all-to-all-done.8 = bf16[4,2,64,1024]{3,1,2,0:T(2,128)(2,1)S(1)} async-done(((bf16[4,2,64,1024]{3,1,2,0:T(2,128)(2,1)}), bf16[4,2,64,1024]{3,1,2,0:T(2,128)(2,1)S(1)}, u32[]{:S(2)}, u32[]{:S(2)}) %all-to-all-start.8) | async-done | bytes 1048608 | tf_op jit(solution)/shard_map/all_to_all | solution.py:150
  77.8 6.7 %all-to-all-start.10 = ((bf16[128,8,512]{0,2,1:T(8,128)(2,1)}), bf16[128,8,512]{0,2,1:T(8,128)(2,1)S(1)}, u32[]{:S(2)}, u32[]{:S(2)}) async-start(bf16[128,8,512]{0,2,1:T(8,128)(2,1)} %bitcast.60), calls=%async_computation.10 | async-start | bytes 2097152 | tf_op jit(solution)/shard_map/all_to_all | solution.py:118
  85.8 24.3 %all-to-all-done.10 = bf16[128,8,512]{0,2,1:T(8,128)(2,1)S(1)} async-done(((bf16[128,8,512]{0,2,1:T(8,128)(2,1)}), bf16[128,8,512]{0,2,1:T(8,128)(2,1)S(1)}, u32[]{:S(2)}, u32[]{:S(2)}) %all-to-all-start.10) | async-done | bytes 1048608 | tf_op jit(solution)/shard_map/all_to_all | solution.py:118
  110.2 3.6 all-to-all-start
  113.7 4.1 copy.137
  117.8 21.8 %all-to-all-done = bf16[128,8,512]{0,2,1:T(8,128)(2,1)S(1)} async-done(((bf16[128,8,512]{0,2,1:T(8,128)(2,1)}), bf16[128,8,512]{0,2,1:T(8,128)(2,1)S(1)}, u32[]{:S(2)}, u32[]{:S(2)}) %all-to-all-start) | async-done | bytes 1048608 | tf_op jit(solution)/shard_map/all_to_all | solution.py:120
  140.6 3.6 all-to-all-start.3
  145.1 4.1 copy.154
  149.1 52.8 %all-to-all-done.3 = bf16[128,8,1024]{0,2,1:T(8,128)(2,1)S(1)} async-done(((bf16[128,8,1024]{0,2,1:T(8,128)(2,1)}), bf16[128,8,1024]{0,2,1:T(8,128)(2,1)S(1)}, u32[]{:S(2)}, u32[]{:S(2)}) %all-to-all-start.3) | async-done | bytes 2097184 | tf_op jit(solution)/shard_map/all_to_all | solution.py:117
  203.2 4.4 all-to-all-start.6
  217.7 47.6 %all-to-all-done.6 = bf16[128,8,1024]{0,2,1:T(8,128)(2,1)} async-done(((bf16[128,8,1024]{0,2,1:T(8,128)(2,1)}), bf16[128,8,1024]{0,2,1:T(8,128)(2,1)}, u32[]{:S(2)}, u32[]{:S(2)}) %all-to-all-start.6) | async-done | bytes 2097184 | tf_op jit(solution)/shard_map/all_to_all | solution.py:116
  265.3 4.5 all-to-all-start.1
  283.8 3.9 copy.138
  287.7 3.9 copy.155
  291.6 3.3 fusion.80
  303.0 65.1 %all-reduce.7.cloned.1.call-done = bf16[1024,64]{0,1:T(8,128)(2,1)} async-done(((bf16[1024,64]{0,1:T(8,128)(2,1)}), bf16[1024,64]{0,1:T(8,128)(2,1)}) %all-reduce.7.cloned.1.call-update) | async-done | bytes 131088 | tf_op jit(solution)/shard_map/psum | solution.py:190
  368.1 3.0 fusion.22
  371.1 50.4 %while.12 = (s32[]{:T(128)}, bf16[2,512,4,128]{3,2,1,0:T(4,128)(2,1)}, s32[2]{0:T(128)S(1)}, bf16[1280,4,128]{2,0,1:T(8,128)(2,1)S(1)}, s32[1024]{0:T(1024)S(1)}...) while((s32[]{:T(128)}, ...), condition=%wide.region_11.13_spmd, body=%wide.region_7.12_spmd.sunk | while | flops 1230110720 | bytes 50923260 | solution.py:93
  375.2 5.1 fusion.110
  382.2 7.7 %fusion.111 = (f32[4,512]{1,0:T(4,128)S(1)}, f32[4,512,768]{2,1,0:T(8,128)S(1)}) fusion(f32[4,512,768]{2,1,0:T(8,128)} %fusion.110, pred[512,768]{1,0:T(8,128)(4,1)S(1)} %compare_and_fusion.4), kind=kOutput, calls=%fused_computation.141.clone.1 | output fusion | flops 9437951 | bytes 12984320 | tf_op jit(solution)/shard_map/while/body/eval_jaxpr/sub | solution.py:79
  389.9 3.4 multiply_reduce_fusion.6
  400.4 5.0 fusion.110
  407.3 7.7 %fusion.111 = (f32[4,512]{1,0:T(4,128)S(1)}, f32[4,512,768]{2,1,0:T(8,128)S(1)}) fusion(f32[4,512,768]{2,1,0:T(8,128)} %fusion.110, pred[512,768]{1,0:T(8,128)(4,1)S(1)} %compare_and_fusion.4), kind=kOutput, calls=%fused_computation.141.clone.1 | output fusion | flops 9437951 | bytes 12984320 | tf_op jit(solution)/shard_map/while/body/eval_jaxpr/sub | solution.py:79
  415.1 3.4 multiply_reduce_fusion.6
  424.5 71.3 %all-reduce.9.cloned.1.call-done = (bf16[1024,64]{0,1:T(8,128)(2,1)}, bf16[1024,64]{0,1:T(8,128)(2,1)}, bf16[1024,64]{0,1:T(8,128)(2,1)}) async-done(((bf16[1024,64]{0,1:T(8,128)(2,1)}, bf16[1024,64]{0,1:T(8,128)(2,1)}, bf16[1024,64]{0,1:T(8,128)(2,1)}), (bf16[1024,64]{0,1:T(8,128)(2,1)}, bf16[1024,64]{0,1:T(8,128)(2,1)}, bf16[1024,64]{0,1:T(8,128)(2,1)})) %all-reduce.9.cloned.1.call-update) | async-done | bytes 393232 | tf_op jit(solution)/shard_map/psum | solution.py:213
  495.8 2.8 broadcast_multiply_fusion
  502.0 4.3 all-to-all-start.9
  510.9 4.3 all-to-all-done.9
  515.2 4.1 all-to-all-start.11
  520.6 2.8 fusion.40
  525.2 3.1 all-to-all-done.11
  528.3 3.5 all-to-all-start.12
  534.3 2.8 fusion.37
  538.8 7.4 %all-to-all-done.12 = bf16[4,2,64,1024]{3,1,2,0:T(2,128)(2,1)S(1)} async-done(((bf16[4,2,64,1024]{3,1,2,0:T(2,128)(2,1)}), bf16[4,2,64,1024]{3,1,2,0:T(2,128)(2,1)S(1)}, u32[]{:S(2)}, u32[]{:S(2)}) %all-to-all-start.12) | async-done | bytes 1048608 | tf_op jit(solution)/shard_map/all_to_all | solution.py:250
  546.2 4.5 all-to-all-start.7
  558.8 2.7 convolution_bitcast_fusion
  561.5 2.5 copy.183
  565.2 4.3 convolution_bitcast_fusion.1
  (159 shorter events, 89.1 us)
Async XLA Ops:
  7.2 23.0 %copy-start = (f32[8,64,1024]{2,1,0:T(8,128)S(1)}, f32[8,64,1024]{2,1,0:T(8,128)}, u32[]{:S(2)}) copy-start(f32[8,64,1024]{2,1,0:T(8,128)} %param.31) | copy-start | bytes 6291460
  7.2 10.1 %copy-start.9 = (f32[8,64,512]{2,1,0:T(8,128)S(1)}, f32[8,64,512]{2,1,0:T(8,128)}, u32[]{:S(2)}) copy-start(f32[8,64,512]{2,1,0:T(8,128)} %param.29) | copy-start | bytes 3145732
  8.7 34.8 %copy-start.26 = (f32[4,2,8]{2,1,0:T(2,128)}, f32[4,2,8]{2,1,0:T(2,128)S(1)}, u32[]{:S(2)}) copy-start(f32[4,2,8]{2,1,0:T(2,128)S(1)} %convert_reduce_fusion.1) | copy-start | bytes 772
  13.1 13.7 %all-to-all-start.4 = ((bf16[4,2,64,512]{3,1,2,0:T(2,128)(2,1)}), bf16[4,2,64,512]{3,1,2,0:T(2,128)(2,1)}, u32[]{:S(2)}, u32[]{:S(2)}) async-start(bf16[4,2,64,512]{3,1,2,0:T(2,128)(2,1)} %copy.141), calls=%async_computation.4 | async-start | bytes 1048576 | tf_op jit(solution)/shard_map/all_to_all | solution.py:152
  26.7 12.3 %all-to-all-start.5 = ((bf16[4,2,64,512]{3,2,1,0:T(8,128)(2,1)}), bf16[4,2,64,512]{3,2,1,0:T(8,128)(2,1)S(1)}, u32[]{:S(2)}, u32[]{:S(2)}) async-start(bf16[4,2,64,512]{3,2,1,0:T(8,128)(2,1)} %copy.151), calls=%async_computation.5 | async-start | bytes 1048576 | tf_op jit(solution)/shard_map/all_to_all | solution.py:151
  39.0 0.8 copy-start.19
  39.8 18.1 %all-to-all-start.2 = ((bf16[4,2,64,1024]{3,1,2,0:T(2,128)(2,1)}), bf16[4,2,64,1024]{3,1,2,0:T(2,128)(2,1)S(1)}, u32[]{:S(2)}, u32[]{:S(2)}) async-start(bf16[4,2,64,1024]{3,1,2,0:T(2,128)(2,1)} %copy.134), calls=%async_computation.2 | async-start | bytes 2097152 | tf_op jit(solution)/shard_map/all_to_all | solution.py:153
  48.9 13.5 %copy-start.10 = (bf16[1,128,4096]{2,1,0:T(8,128)(2,1)S(1)}, bf16[1,128,4096]{2,1,0:T(8,128)(2,1)}, u32[]{:S(2)}) copy-start(bf16[1,128,4096]{2,1,0:T(8,128)(2,1)} %param.20) | copy-start | bytes 3145732
  57.9 1.0 copy-start.15
  58.9 18.0 %all-to-all-start.8 = ((bf16[4,2,64,1024]{3,1,2,0:T(2,128)(2,1)}), bf16[4,2,64,1024]{3,1,2,0:T(2,128)(2,1)S(1)}, u32[]{:S(2)}, u32[]{:S(2)}) async-start(bf16[4,2,64,1024]{3,1,2,0:T(2,128)(2,1)} %copy.162), calls=%async_computation.8 | async-start | bytes 2097152 | tf_op jit(solution)/shard_map/all_to_all | solution.py:150
  62.5 22.1 %copy-start.11 = (bf16[1,128,4096]{2,1,0:T(8,128)(2,1)S(1)}, bf16[1,128,4096]{2,1,0:T(8,128)(2,1)}, u32[]{:S(2)}) copy-start(bf16[1,128,4096]{2,1,0:T(8,128)(2,1)} %param.22) | copy-start | bytes 3145732
  76.9 1.0 copy-start.13
  77.8 32.3 %all-to-all-start.10 = ((bf16[128,8,512]{0,2,1:T(8,128)(2,1)}), bf16[128,8,512]{0,2,1:T(8,128)(2,1)S(1)}, u32[]{:S(2)}, u32[]{:S(2)}) async-start(bf16[128,8,512]{0,2,1:T(8,128)(2,1)} %bitcast.60), calls=%async_computation.10 | async-start | bytes 2097152 | tf_op jit(solution)/shard_map/all_to_all | solution.py:118
  110.2 29.4 %all-to-all-start = ((bf16[128,8,512]{0,2,1:T(8,128)(2,1)}), bf16[128,8,512]{0,2,1:T(8,128)(2,1)S(1)}, u32[]{:S(2)}, u32[]{:S(2)}) async-start(bf16[128,8,512]{0,2,1:T(8,128)(2,1)} %bitcast.10), calls=%async_computation | async-start | bytes 2097152 | tf_op jit(solution)/shard_map/all_to_all | solution.py:120
  139.6 1.0 copy-start.4
  139.6 4.6 copy-start.24
  140.6 61.3 %all-to-all-start.3 = ((bf16[128,8,1024]{0,2,1:T(8,128)(2,1)}), bf16[128,8,1024]{0,2,1:T(8,128)(2,1)S(1)}, u32[]{:S(2)}, u32[]{:S(2)}) async-start(bf16[128,8,1024]{0,2,1:T(8,128)(2,1)} %bitcast.184), calls=%async_computation.3 | async-start | bytes 4194304 | tf_op jit(solution)/shard_map/all_to_all | solution.py:117
  144.2 131.8 %all-gather.5.cloned.1.call-start = ((), (), s32[]{:S(2)}) async-start(), calls=%async_computation.14 | async-start | bytes 1179648 | tf_op jit(solution)/shard_map/all_gather | solution.py:126
  201.9 1.3 copy-start.2
  201.9 5.7 copy-start.25
  201.9 6.5 %copy-start.28 = (s32[1,8]{1,0:T(1,128)S(1)}, s32[1,8]{1,0:T(1,128)}, u32[]{:S(2)}) copy-start(s32[1,8]{1,0:T(1,128)} %param.25) | copy-start | bytes 100
  203.2 62.1 %all-to-all-start.6 = ((bf16[128,8,1024]{0,2,1:T(8,128)(2,1)}), bf16[128,8,1024]{0,2,1:T(8,128)(2,1)}, u32[]{:S(2)}, u32[]{:S(2)}) async-start(bf16[128,8,1024]{0,2,1:T(8,128)(2,1)} %bitcast.183), calls=%async_computation.6 | async-start | bytes 4194304 | tf_op jit(solution)/shard_map/all_to_all | solution.py:116
  207.6 70.1 %all-gather.7.cloned.1.call-start = ((), (), s32[]{:S(2)}) async-start(), calls=%async_computation.15 | async-start | bytes 1179648 | tf_op jit(solution)/shard_map/all_gather | solution.py:127
  208.7 5.4 copy-start.20
  211.0 4.5 copy-start.16
  213.0 1.0 copy-start.21
  215.5 54.8 %copy-start.14 = (bf16[4,2,64,1024]{3,1,2,0:T(2,128)(2,1)S(1)}, bf16[4,2,64,1024]{3,1,2,0:T(2,128)(2,1)}, u32[]{:S(2)}) copy-start(bf16[4,2,64,1024]{3,1,2,0:T(2,128)(2,1)} %copy-done.13) | copy-start | bytes 3145732
  265.3 6.2 %copy-start.18 = (bf16[8,64,1024]{2,0,1:T(8,128)(2,1)S(1)}, bf16[8,64,1024]{2,0,1:T(8,128)(2,1)}, u32[]{:S(2)}) copy-start(bf16[8,64,1024]{2,0,1:T(8,128)(2,1)} %bitcast_convert_fusion.1) | copy-start | bytes 3145732
  265.3 37.7 %all-to-all-start.1 = ((bf16[128,8,512]{0,2,1:T(8,128)(2,1)}), bf16[128,8,512]{0,2,1:T(8,128)(2,1)}, u32[]{:S(2)}, u32[]{:S(2)}) async-start(bf16[128,8,512]{0,2,1:T(8,128)(2,1)} %bitcast.12), calls=%async_computation.1 | async-start | bytes 2097152 | tf_op jit(solution)/shard_map/all_to_all | solution.py:119
  269.9 98.3 %all-reduce.7.cloned.1.call-start = ((), (), s32[]{:S(2)}) async-start(), calls=%async_computation.13 | async-start | bytes 262144 | tf_op jit(solution)/shard_map/psum | solution.py:190
  291.6 3.4 copy-start.6
  291.6 3.4 copy-start.17
  297.9 197.9 %all-reduce.9.cloned.1.call-start = ((), (), s32[]{:S(2)}) async-start(), calls=%async_computation.16 | async-start | bytes 786432 | tf_op jit(solution)/shard_map/psum | solution.py:213
  299.5 1.4 copy-start.5
  300.9 67.2 %copy-start.22 = (bf16[8,64,512]{2,0,1:T(8,128)(2,1)S(1)}, bf16[8,64,512]{2,0,1:T(8,128)(2,1)}, u32[]{:S(2)}) copy-start(bf16[8,64,512]{2,0,1:T(8,128)(2,1)} %copy-done.21) | copy-start | bytes 1572868
  421.5 1.5 copy-start.29
  423.0 72.8 %copy-start.23 = (bf16[1024,64]{0,1:T(8,128)(2,1)S(1)}, bf16[1024,64]{0,1:T(8,128)(2,1)}, u32[]{:S(2)}) copy-start(bf16[1024,64]{0,1:T(8,128)(2,1)} %all-reduce.7.cloned.1.call-done) | copy-start | bytes 393220
  495.8 2.8 copy-start.12
  499.3 7.0 %copy-start.3 = (bf16[8,128,512]{2,1,0:T(8,128)(2,1)S(1)}, bf16[8,128,512]{2,1,0:T(8,128)(2,1)}, u32[]{:S(2)}) copy-start(bf16[8,128,512]{2,1,0:T(8,128)(2,1)} %copy.170) | copy-start | bytes 3145732
  502.0 13.2 %all-to-all-start.9 = ((bf16[4,2,64,512]{3,1,2,0:T(2,128)(2,1)}), bf16[4,2,64,512]{3,1,2,0:T(2,128)(2,1)}, u32[]{:S(2)}, u32[]{:S(2)}) async-start(bf16[4,2,64,512]{3,1,2,0:T(2,128)(2,1)} %copy.166), calls=%async_computation.9 | async-start | bytes 1048576 | tf_op jit(solution)/shard_map/all_to_all | solution.py:236
  508.3 11.1 %copy-start.8 = (bf16[8,128,1024]{2,1,0:T(8,128)(2,1)S(1)}, bf16[8,128,1024]{2,1,0:T(8,128)(2,1)}, u32[]{:S(2)}) copy-start(bf16[8,128,1024]{2,1,0:T(8,128)(2,1)} %copy.138) | copy-start | bytes 6291460
  515.2 13.0 %all-to-all-start.11 = ((bf16[4,2,64,512]{3,1,2,0:T(2,128)(2,1)}), bf16[4,2,64,512]{3,1,2,0:T(2,128)(2,1)}, u32[]{:S(2)}, u32[]{:S(2)}) async-start(bf16[4,2,64,512]{3,1,2,0:T(2,128)(2,1)} %copy.172), calls=%async_computation.11 | async-start | bytes 1048576 | tf_op jit(solution)/shard_map/all_to_all | solution.py:243
  525.2 6.6 %copy-start.7 = (bf16[8,128,1024]{2,1,0:T(8,128)(2,1)S(1)}, bf16[8,128,1024]{2,1,0:T(8,128)(2,1)}, u32[]{:S(2)}) copy-start(bf16[8,128,1024]{2,1,0:T(8,128)(2,1)} %copy.155) | copy-start | bytes 6291460
  528.3 18.0 %all-to-all-start.12 = ((bf16[4,2,64,1024]{3,1,2,0:T(2,128)(2,1)}), bf16[4,2,64,1024]{3,1,2,0:T(2,128)(2,1)S(1)}, u32[]{:S(2)}, u32[]{:S(2)}) async-start(bf16[4,2,64,1024]{3,1,2,0:T(2,128)(2,1)} %copy.177), calls=%async_computation.12 | async-start | bytes 2097152 | tf_op jit(solution)/shard_map/all_to_all | solution.py:250
  537.1 13.7 %copy-start.27 = (f32[4,2,8]{2,1,0:T(2,128)S(1)}, f32[4,2,8]{2,1,0:T(2,128)}, u32[]{:S(2)}) copy-start(f32[4,2,8]{2,1,0:T(2,128)} %copy-done.26) | copy-start | bytes 772
  546.2 19.0 %all-to-all-start.7 = ((bf16[4,2,64,1024]{3,1,2,0:T(2,128)(2,1)}), bf16[4,2,64,1024]{3,1,2,0:T(2,128)(2,1)}, u32[]{:S(2)}, u32[]{:S(2)}) async-start(bf16[4,2,64,1024]{3,1,2,0:T(2,128)(2,1)} %copy.157), calls=%async_computation.7 | async-start | bytes 2097152 | tf_op jit(solution)/shard_map/all_to_all | solution.py:229
  565.2 6.8 %copy-start.1 = (f32[8,64,1024]{2,1,0:T(8,128)S(1)}, f32[8,64,1024]{2,1,0:T(8,128)}, u32[]{:S(2)}) copy-start(f32[8,64,1024]{2,1,0:T(8,128)} %param.31) | copy-start | bytes 6291460
Sparse Core Ops, SparseCore 0:
  147.1 61.6 all-gather.4
  210.9 61.0 all-gather.6
  298.0 70.0 all-reduce.6
  424.6 71.1 all-reduce.8
where the time goes:
time: 588 us; the launch traced here: 579 us
  waiting for transfers between devices  329 us (56%)
  matrix products  79.1 us (13%)
  local copies, waits for them, and re-layouts  67.7 us (12%)
  starting transfers between devices  54.7 us (9%)
  other arithmetic  25.2 us (4%)
  between operations  14.8 us (3%)
  loops' own time  8.21 us (1%)
    psum x1, waiting for transfers between devices, shards(): low_rank_back = lax.psum(partial_back.astype(jnp.bfloat16), 'seq')  71.3 us
    psum x1, waiting for transfers between devices, shards(): lax.psum(partial_grad.astype(jnp.bfloat16), 'seq').astype(jnp.float32)  65.1 us
    all_to_all x1, waiting for transfers between devices, shards(): lax.all_to_all(out_grad[0], 'seq', split_axis=1, concat_axis=0, tiled=True)  52.8 us
    all_to_all x1, waiting for transfers between devices, shards(): lax.all_to_all(layer_input[0], 'seq', split_axis=1, concat_axis=0, tiled=...  47.6 us
    unnamed x71, local copies, waits for them, and re-layouts  28.1 us
    all_to_all x1, waiting for transfers between devices, shards(): lax.all_to_all(attention_out[0], 'seq', split_axis=1, concat_axis=0, tile...  24.3 us
    all_to_all x1, waiting for transfers between devices, shards(): lax.all_to_all(query_rows[0], 'seq', split_axis=1, concat_axis=0, tiled=T...  21.8 us
    sub x2, other arithmetic, one_block(): weights = jnp.exp(scores - row_max)  15.4 us
  transfers between devices with their start and end apart: 17, of which 14 were waited for; matrix products, arithmetic and copies ran while one was open for 17% of the time, Pallas kernels for 0%

commit v1 on v0

--- a/solution.py
+++ b/solution.py
@@ -11,6 +11,22 @@
 adapter_scale = 2.0
 big_negative = -1e30
 highest = lax.Precision.HIGHEST
+
+
+def swapped_with_each(x, axis, split, join):
+    ways, here = (lax.axis_size(axis), lax.axis_index(axis))
+    width = x.shape[split] // ways
+    dims = list(x.shape)
+    dims[split] = width
+    height = dims[join]
+    dims[join] = height * ways
+    full = jnp.zeros(dims, x.dtype)
+    for mask in range(ways):
+        part = lax.dynamic_slice_in_dim(x, (here ^ mask) * width, width, axis=split)
+        if mask:
+            part = lax.ppermute(part, axis, [(d, d ^ mask) for d in range(ways)])
+        full = lax.dynamic_update_slice_in_dim(full, part, (here ^ mask) * height, axis=join)
+    return full
 
 
 def contract_axes(left_side, right_side, left_dim, right_dim):
@@ -147,7 +163,7 @@
         )
 
     fetched = (
-        lax.all_to_all(pack_slots(query_down), "head", split_axis=0, concat_axis=0, tiled=True),
+        swapped_with_each(pack_slots(query_down), "head", 0, 0),
         lax.all_to_all(pack_slots(query_up), "head", split_axis=0, concat_axis=0, tiled=True),
         lax.all_to_all(pack_slots(output_down), "head", split_axis=0, concat_axis=0, tiled=True),
         lax.all_to_all(pack_slots(output_up), "head", split_axis=0, concat_axis=0, tiled=True),

time: 588 us -> 576 us (0.980)
  waiting for transfers between devices: 329 us -> 301 us
  local copies, waits for them, and re-layouts: 67.7 us -> 86.9 us
    all_to_all x1, waiting for transfers between devices: 52.8 us -> 6.77 us  [shards(): lax.all_to_all(out_grad[0], 'seq', split_axis=1, concat_axis=0, tiled=True)]
    dynamic_update_slice x0 -> x4, local copies, waits for them, and re-layouts: none -> 13.5 us  [swapped_with_each(): lax.dynamic_update_slice_in_dim(full, part, (here ^ mask) * height, axis=...]
    all_to_all x1 -> x0, waiting for transfers between devices: 13.1 us -> none  [shards(): lax.all_to_all(pack_slots(query_down), 'head', split_axis=0, concat_axis=...]
    all_gather x1, waiting for transfers between devices: 0.02 us -> 9.87 us  [shards(): lax.all_gather(value_rows[0], 'seq', axis=0, tiled=True)]
    ppermute x0 -> x3, waiting for transfers between devices: none -> 6.48 us  [swapped_with_each(): part = lax.ppermute(part, axis, [(d, d ^ mask) for d in range(ways)])]
    all_to_all x1, waiting for transfers between devices: 7.22 us -> 13.1 us  [shards(): lax.all_to_all(pack_slots(output_up), 'head', split_axis=0, concat_axis=0...]
    unnamed x71 -> x63, local copies, waits for them, and re-layouts: 28.1 us -> 26.4 us
  transfers between devices with their start and end apart: 17 -> 19, of which waited for: 14 -> 16; matrix products, arithmetic and copies ran while one was open for 17% -> 21% of each run, Pallas kernels for 0% -> 0%
where the time goes in v1:
time: 576 us; the launch traced here: 566 us
  waiting for transfers between devices  301 us (52%)
  local copies, waits for them, and re-layouts  86.9 us (15%)
  matrix products  77.7 us (13%)
  starting transfers between devices  52.4 us (9%)
  other arithmetic  25.1 us (4%)
  between operations  14.9 us (3%)
  loops' own time  7.6 us (1%)
    psum x1, waiting for transfers between devices, shards(): low_rank_back = lax.psum(partial_back.astype(jnp.bfloat16), 'seq')  71.3 us
    psum x1, waiting for transfers between devices, shards(): lax.psum(partial_grad.astype(jnp.bfloat16), 'seq').astype(jnp.float32)  68.7 us
    all_to_all x1, waiting for transfers between devices, shards(): lax.all_to_all(layer_input[0], 'seq', split_axis=1, concat_axis=0, tiled=...  52.8 us
    unnamed x63, local copies, waits for them, and re-layouts  26.4 us
    all_to_all x1, waiting for transfers between devices, shards(): lax.all_to_all(attention_out[0], 'seq', split_axis=1, concat_axis=0, tile...  24.3 us
    all_to_all x1, waiting for transfers between devices, shards(): lax.all_to_all(query_rows[0], 'seq', split_axis=1, concat_axis=0, tiled=T...  21.8 us
    sub x2, other arithmetic, one_block(): weights = jnp.exp(scores - row_max)  15.4 us
    dot_general x8, matrix products, contract_axes(): lax.dot_general(left_side, right_side, (((left_dim,), (right_dim,)), ((),...  14.5 us
  transfers between devices with their start and end apart: 19, of which 16 were waited for; matrix products, arithmetic and copies ran while one was open for 21% of the time, Pallas kernels for 0%

profile of v1, /device:TPU:0, one launch (start us, length us, event | category | flops | bytes accessed | tf_op | source)
XLA Modules:
  0.0 565.7 jit_solution(8817174560100492129)
XLA Ops:
  8.7 3.1 convolution_convert_fusion.1
  13.0 4.2 all-to-all-start.4
  20.0 6.7 %all-to-all-done.4 = bf16[4,2,64,512]{3,1,2,0:T(2,128)(2,1)} async-done(((bf16[4,2,64,512]{3,1,2,0:T(2,128)(2,1)}), bf16[4,2,64,512]{3,1,2,0:T(2,128)(2,1)}, u32[]{:S(2)}, u32[]{:S(2)}) %all-to-all-start.4) | async-done | bytes 524320 | tf_op jit(solution)/shard_map/all_to_all | solution.py:168
  26.7 3.5 all-to-all-start.5
  30.2 3.8 fusion.32
  35.8 3.2 all-to-all-done.5
  39.8 3.5 all-to-all-start.2
  44.7 13.1 %all-to-all-done.2 = bf16[4,2,64,1024]{3,1,2,0:T(2,128)(2,1)S(1)} async-done(((bf16[4,2,64,1024]{3,1,2,0:T(2,128)(2,1)}), bf16[4,2,64,1024]{3,1,2,0:T(2,128)(2,1)S(1)}, u32[]{:S(2)}, u32[]{:S(2)}) %all-to-all-start.2) | async-done | bytes 1048608 | tf_op jit(solution)/shard_map/all_to_all | solution.py:169
  58.7 6.7 %all-to-all-start.9 = ((bf16[128,8,512]{0,2,1:T(8,128)(2,1)}), bf16[128,8,512]{0,2,1:T(8,128)(2,1)S(1)}, u32[]{:S(2)}, u32[]{:S(2)}) async-start(bf16[128,8,512]{0,2,1:T(8,128)(2,1)} %bitcast.60), calls=%async_computation.9 | async-start | bytes 2097152 | tf_op jit(solution)/shard_map/all_to_all | solution.py:134
  66.7 24.3 %all-to-all-done.9 = bf16[128,8,512]{0,2,1:T(8,128)(2,1)S(1)} async-done(((bf16[128,8,512]{0,2,1:T(8,128)(2,1)}), bf16[128,8,512]{0,2,1:T(8,128)(2,1)S(1)}, u32[]{:S(2)}, u32[]{:S(2)}) %all-to-all-start.9) | async-done | bytes 1048608 | tf_op jit(solution)/shard_map/all_to_all | solution.py:134
  91.1 3.6 all-to-all-start
  94.6 4.1 copy.170
  98.7 21.8 %all-to-all-done = bf16[128,8,512]{0,2,1:T(8,128)(2,1)S(1)} async-done(((bf16[128,8,512]{0,2,1:T(8,128)(2,1)}), bf16[128,8,512]{0,2,1:T(8,128)(2,1)S(1)}, u32[]{:S(2)}, u32[]{:S(2)}) %all-to-all-start) | async-done | bytes 1048608 | tf_op jit(solution)/shard_map/all_to_all | solution.py:136
  121.5 3.6 all-to-all-start.6
  126.0 4.1 copy.153
  130.0 52.8 %all-to-all-done.6 = bf16[128,8,1024]{0,2,1:T(8,128)(2,1)S(1)} async-done(((bf16[128,8,1024]{0,2,1:T(8,128)(2,1)}), bf16[128,8,1024]{0,2,1:T(8,128)(2,1)S(1)}, u32[]{:S(2)}, u32[]{:S(2)}) %all-to-all-start.6) | async-done | bytes 2097184 | tf_op jit(solution)/shard_map/all_to_all | solution.py:132
  184.1 4.6 all-to-all-start.3
  188.8 5.4 fusion.35
  194.2 3.2 constant_dynamic-slice_fusion.5
  203.0 3.4 dynamic_update_slice.19
  208.0 3.4 dynamic_update_slice.20
  214.0 3.4 dynamic_update_slice.21
  217.4 5.5 collective-permute-done.2
  224.4 3.4 dynamic_update_slice.22
  234.4 6.8 %all-to-all-done.3 = bf16[128,8,1024]{0,2,1:T(8,128)(2,1)} async-done(((bf16[128,8,1024]{0,2,1:T(8,128)(2,1)}), bf16[128,8,1024]{0,2,1:T(8,128)(2,1)}, u32[]{:S(2)}, u32[]{:S(2)}) %all-to-all-start.3) | async-done | bytes 2097184 | tf_op jit(solution)/shard_map/all_to_all | solution.py:133
  241.2 4.3 all-to-all-start.1
  251.7 9.9 %all-gather.7.cloned.1.call-done = bf16[1,1024,512]{1,2,0:T(8,128)(2,1)} async-done(((bf16[1,128,512]{1,2,0:T(8,128)(2,1)}), bf16[1,1024,512]{1,2,0:T(8,128)(2,1)}) %all-gather.7.cloned.1.call-update) | async-done | bytes 1048592 | tf_op jit(solution)/shard_map/all_gather | solution.py:143
  267.7 3.9 copy.171
  271.7 3.9 copy.154
  275.6 3.3 fusion.82
  286.9 68.7 %all-reduce.7.cloned.1.call-done = bf16[1024,64]{0,1:T(8,128)(2,1)} async-done(((bf16[1024,64]{0,1:T(8,128)(2,1)}), bf16[1024,64]{0,1:T(8,128)(2,1)}) %all-reduce.7.cloned.1.call-update) | async-done | bytes 131088 | tf_op jit(solution)/shard_map/psum | solution.py:206
  355.6 3.0 fusion.22
  358.6 49.6 %while.12 = (s32[]{:T(128)}, bf16[2,512,4,128]{3,2,1,0:T(4,128)(2,1)}, s32[2]{0:T(128)S(1)}, bf16[1280,4,128]{2,0,1:T(8,128)(2,1)S(1)}, s32[1024]{0:T(1024)S(1)}...) while((s32[]{:T(128)}, ...), condition=%wide.region_11.13_spmd, body=%wide.region_7.12_spmd.sunk | while | flops 1230110720 | bytes 50923260 | solution.py:109
  362.3 5.1 fusion.112
  369.2 7.7 %fusion.113 = (f32[4,512]{1,0:T(4,128)S(1)}, f32[4,512,768]{2,1,0:T(8,128)S(1)}) fusion(f32[4,512,768]{2,1,0:T(8,128)} %fusion.112, pred[512,768]{1,0:T(8,128)(4,1)S(1)} %compare_and_fusion.4), kind=kOutput, calls=%fused_computation.146.clone.1 | output fusion | flops 9437951 | bytes 12984320 | tf_op jit(solution)/shard_map/while/body/eval_jaxpr/sub | solution.py:95
  377.0 3.4 multiply_reduce_fusion.6
  387.1 5.1 fusion.112
  394.0 7.7 %fusion.113 = (f32[4,512]{1,0:T(4,128)S(1)}, f32[4,512,768]{2,1,0:T(8,128)S(1)}) fusion(f32[4,512,768]{2,1,0:T(8,128)} %fusion.112, pred[512,768]{1,0:T(8,128)(4,1)S(1)} %compare_and_fusion.4), kind=kOutput, calls=%fused_computation.146.clone.1 | output fusion | flops 9437951 | bytes 12984320 | tf_op jit(solution)/shard_map/while/body/eval_jaxpr/sub | solution.py:95
  401.7 3.4 multiply_reduce_fusion.6
  411.2 71.3 %all-reduce.9.cloned.1.call-done = (bf16[1024,64]{0,1:T(8,128)(2,1)}, bf16[1024,64]{0,1:T(8,128)(2,1)}, bf16[1024,64]{0,1:T(8,128)(2,1)}) async-done(((bf16[1024,64]{0,1:T(8,128)(2,1)}, bf16[1024,64]{0,1:T(8,128)(2,1)}, bf16[1024,64]{0,1:T(8,128)(2,1)}), (bf16[1024,64]{0,1:T(8,128)(2,1)}, bf16[1024,64]{0,1:T(8,128)(2,1)}, bf16[1024,64]{0,1:T(8,128)(2,1)})) %all-reduce.9.cloned.1.call-update) | async-done | bytes 393232 | tf_op jit(solution)/shard_map/psum | solution.py:229
  488.6 4.4 all-to-all-start.8
  497.6 4.3 all-to-all-done.8
  501.9 4.1 all-to-all-start.10
  511.9 3.1 all-to-all-done.10
  514.9 3.5 all-to-all-start.11
  525.5 7.4 %all-to-all-done.11 = bf16[4,2,64,1024]{3,1,2,0:T(2,128)(2,1)S(1)} async-done(((bf16[4,2,64,1024]{3,1,2,0:T(2,128)(2,1)}), bf16[4,2,64,1024]{3,1,2,0:T(2,128)(2,1)S(1)}, u32[]{:S(2)}, u32[]{:S(2)}) %all-to-all-start.11) | async-done | bytes 1048608 | tf_op jit(solution)/shard_map/all_to_all | solution.py:266
  532.9 4.5 all-to-all-start.7
  551.9 4.3 convolution_bitcast_fusion.1
  (164 shorter events, 106.2 us)
Async XLA Ops:
  7.2 23.0 %copy-start = (f32[8,64,1024]{2,1,0:T(8,128)S(1)}, f32[8,64,1024]{2,1,0:T(8,128)}, u32[]{:S(2)}) copy-start(f32[8,64,1024]{2,1,0:T(8,128)} %param.31) | copy-start | bytes 6291460
  7.2 10.1 %copy-start.9 = (f32[8,64,512]{2,1,0:T(8,128)S(1)}, f32[8,64,512]{2,1,0:T(8,128)}, u32[]{:S(2)}) copy-start(f32[8,64,512]{2,1,0:T(8,128)} %param.29) | copy-start | bytes 3145732
  13.0 13.7 %all-to-all-start.4 = ((bf16[4,2,64,512]{3,1,2,0:T(2,128)(2,1)}), bf16[4,2,64,512]{3,1,2,0:T(2,128)(2,1)}, u32[]{:S(2)}, u32[]{:S(2)}) async-start(bf16[4,2,64,512]{3,1,2,0:T(2,128)(2,1)} %copy.157), calls=%async_computation.4 | async-start | bytes 1048576 | tf_op jit(solution)/shard_map/all_to_all | solution.py:168
  26.7 12.3 %all-to-all-start.5 = ((bf16[4,2,64,512]{3,2,1,0:T(8,128)(2,1)}), bf16[4,2,64,512]{3,2,1,0:T(8,128)(2,1)S(1)}, u32[]{:S(2)}, u32[]{:S(2)}) async-start(bf16[4,2,64,512]{3,2,1,0:T(8,128)(2,1)} %copy.167), calls=%async_computation.5 | async-start | bytes 1048576 | tf_op jit(solution)/shard_map/all_to_all | solution.py:167
  34.0 9.3 %copy-start.10 = (bf16[1,128,4096]{2,1,0:T(8,128)(2,1)S(1)}, bf16[1,128,4096]{2,1,0:T(8,128)(2,1)}, u32[]{:S(2)}) copy-start(bf16[1,128,4096]{2,1,0:T(8,128)(2,1)} %param.20) | copy-start | bytes 3145732
  39.0 0.8 copy-start.17
  39.8 18.0 %all-to-all-start.2 = ((bf16[4,2,64,1024]{3,1,2,0:T(2,128)(2,1)}), bf16[4,2,64,1024]{3,1,2,0:T(2,128)(2,1)S(1)}, u32[]{:S(2)}, u32[]{:S(2)}) async-start(bf16[4,2,64,1024]{3,1,2,0:T(2,128)(2,1)} %copy.150), calls=%async_computation.2 | async-start | bytes 2097152 | tf_op jit(solution)/shard_map/all_to_all | solution.py:169
  43.3 22.1 %copy-start.11 = (bf16[1,128,4096]{2,1,0:T(8,128)(2,1)S(1)}, bf16[1,128,4096]{2,1,0:T(8,128)(2,1)}, u32[]{:S(2)}) copy-start(bf16[1,128,4096]{2,1,0:T(8,128)(2,1)} %param.22) | copy-start | bytes 3145732
  57.8 1.0 copy-start.13
  58.7 32.3 %all-to-all-start.9 = ((bf16[128,8,512]{0,2,1:T(8,128)(2,1)}), bf16[128,8,512]{0,2,1:T(8,128)(2,1)S(1)}, u32[]{:S(2)}, u32[]{:S(2)}) async-start(bf16[128,8,512]{0,2,1:T(8,128)(2,1)} %bitcast.60), calls=%async_computation.9 | async-start | bytes 2097152 | tf_op jit(solution)/shard_map/all_to_all | solution.py:134
  91.1 29.4 %all-to-all-start = ((bf16[128,8,512]{0,2,1:T(8,128)(2,1)}), bf16[128,8,512]{0,2,1:T(8,128)(2,1)S(1)}, u32[]{:S(2)}, u32[]{:S(2)}) async-start(bf16[128,8,512]{0,2,1:T(8,128)(2,1)} %bitcast.10), calls=%async_computation | async-start | bytes 2097152 | tf_op jit(solution)/shard_map/all_to_all | solution.py:136
  120.5 1.0 copy-start.4
  120.5 4.6 copy-start.22
  121.5 61.3 %all-to-all-start.6 = ((bf16[128,8,1024]{0,2,1:T(8,128)(2,1)}), bf16[128,8,1024]{0,2,1:T(8,128)(2,1)S(1)}, u32[]{:S(2)}, u32[]{:S(2)}) async-start(bf16[128,8,1024]{0,2,1:T(8,128)(2,1)} %bitcast.187), calls=%async_computation.6 | async-start | bytes 4194304 | tf_op jit(solution)/shard_map/all_to_all | solution.py:132
  125.1 125.0 %all-gather.5.cloned.1.call-start = ((), (), s32[]{:S(2)}) async-start(), calls=%async_computation.13 | async-start | bytes 1179648 | tf_op jit(solution)/shard_map/all_gather | solution.py:142
  182.8 1.3 copy-start.2
  184.1 57.0 %all-to-all-start.3 = ((bf16[128,8,1024]{0,2,1:T(8,128)(2,1)}), bf16[128,8,1024]{0,2,1:T(8,128)(2,1)}, u32[]{:S(2)}, u32[]{:S(2)}) async-start(bf16[128,8,1024]{0,2,1:T(8,128)(2,1)} %bitcast.186), calls=%async_computation.3 | async-start | bytes 4194304 | tf_op jit(solution)/shard_map/all_to_all | solution.py:133
  188.7 72.9 %all-gather.7.cloned.1.call-start = ((), (), s32[]{:S(2)}) async-start(), calls=%async_computation.14 | async-start | bytes 1179648 | tf_op jit(solution)/shard_map/all_gather | solution.py:143
  194.2 5.1 copy-start.23
  194.2 5.8 %copy-start.24 = (s32[1,8]{1,0:T(1,128)S(1)}, s32[1,8]{1,0:T(1,128)}, u32[]{:S(2)}) copy-start(s32[1,8]{1,0:T(1,128)} %param.25) | copy-start | bytes 100
  197.4 3.6 copy-start.12
  197.4 9.1 %collective-permute-start = (bf16[1,2,64,1024]{3,0,2,1:T(2,128)(2,1)}, bf16[1,2,64,1024]{3,0,2,1:T(2,128)(2,1)}, u32[]{:S(2)}, u32[]{:S(2)}) collective-permute-start(bf16[1,2,64,1024]{3,0,2,1:T(2,128)(2,1)} %get-tuple-element.216), channel_id=1, source_target_pairs={{0,1},{1,0},{2,3},{3,2},{4,5},{5,4},{6,7},{7,6},{8,9},{9,8},{10,11... | collective-permute-start | bytes 786440 | tf_op jit(solution)/shard_map/ppermute | solution.py:27
  197.4 15.0 %collective-permute-start.1 = (bf16[1,2,64,1024]{3,0,2,1:T(2,128)(2,1)}, bf16[1,2,64,1024]{3,0,2,1:T(2,128)(2,1)}, u32[]{:S(2)}, u32[]{:S(2)}) collective-permute-start(bf16[1,2,64,1024]{3,0,2,1:T(2,128)(2,1)} %get-tuple-element.215), channel_id=1, source_target_pairs={{0,2},{1,3},{2,0},{3,1},{4,6},{5,7},{6,4},{7,5},{8,10},{9,11},{10,... | collective-permute-start | bytes 786440 | tf_op jit(solution)/shard_map/ppermute | solution.py:27
  198.7 24.1 %collective-permute-start.2 = (bf16[1,2,64,1024]{3,0,2,1:T(2,128)(2,1)}, bf16[1,2,64,1024]{3,0,2,1:T(2,128)(2,1)}, u32[]{:S(2)}, u32[]{:S(2)}) collective-permute-start(bf16[1,2,64,1024]{3,0,2,1:T(2,128)(2,1)} %get-tuple-element.214), channel_id=1, source_target_pairs={{0,3},{1,2},{2,1},{3,0},{4,7},{5,6},{6,5},{7,4},{8,11},{9,10},{10,... | collective-permute-start | bytes 786440 | tf_op jit(solution)/shard_map/ppermute | solution.py:27
  228.6 4.3 copy-start.18
  231.9 9.2 %copy-start.19 = (bf16[8,64,512]{2,0,1:T(8,128)(2,1)}, bf16[8,64,512]{2,0,1:T(8,128)(2,1)S(1)}, u32[]{:S(2)}) copy-start(bf16[8,64,512]{2,0,1:T(8,128)(2,1)S(1)} %fusion.44) | copy-start | bytes 1572868
  231.9 13.5 %copy-start.14 = (bf16[4,2,64,1024]{3,1,2,0:T(2,128)(2,1)S(1)}, bf16[4,2,64,1024]{3,1,2,0:T(2,128)(2,1)}, u32[]{:S(2)}) copy-start(bf16[4,2,64,1024]{3,1,2,0:T(2,128)(2,1)} %copy-done.13) | copy-start | bytes 3145732
  241.2 45.7 %all-to-all-start.1 = ((bf16[128,8,512]{0,2,1:T(8,128)(2,1)}), bf16[128,8,512]{0,2,1:T(8,128)(2,1)}, u32[]{:S(2)}, u32[]{:S(2)}) async-start(bf16[128,8,512]{0,2,1:T(8,128)(2,1)} %bitcast.12), calls=%async_computation.1 | async-start | bytes 2097152 | tf_op jit(solution)/shard_map/all_to_all | solution.py:135
  245.4 110.1 %all-reduce.7.cloned.1.call-start = ((), (), s32[]{:S(2)}) async-start(), calls=%async_computation.12 | async-start | bytes 262144 | tf_op jit(solution)/shard_map/psum | solution.py:206
  275.6 3.3 copy-start.7
  275.6 3.4 copy-start.16
  281.8 200.7 %all-reduce.9.cloned.1.call-start = ((), (), s32[]{:S(2)}) async-start(), calls=%async_computation.15 | async-start | bytes 786432 | tf_op jit(solution)/shard_map/psum | solution.py:229
  283.4 1.4 copy-start.5
  284.8 70.8 %copy-start.20 = (bf16[8,64,512]{2,0,1:T(8,128)(2,1)S(1)}, bf16[8,64,512]{2,0,1:T(8,128)(2,1)}, u32[]{:S(2)}) copy-start(bf16[8,64,512]{2,0,1:T(8,128)(2,1)} %copy-done.19) | copy-start | bytes 1572868
  408.2 1.5 copy-start.25
  409.7 72.8 %copy-start.21 = (bf16[1024,64]{0,1:T(8,128)(2,1)S(1)}, bf16[1024,64]{0,1:T(8,128)(2,1)}, u32[]{:S(2)}) copy-start(bf16[1024,64]{0,1:T(8,128)(2,1)} %all-reduce.7.cloned.1.call-done) | copy-start | bytes 393220
  482.5 2.8 copy-start.15
  486.0 7.0 %copy-start.3 = (bf16[8,128,512]{2,1,0:T(8,128)(2,1)S(1)}, bf16[8,128,512]{2,1,0:T(8,128)(2,1)}, u32[]{:S(2)}) copy-start(bf16[8,128,512]{2,1,0:T(8,128)(2,1)} %copy.188) | copy-start | bytes 3145732
  488.6 13.3 %all-to-all-start.8 = ((bf16[4,2,64,512]{3,1,2,0:T(2,128)(2,1)}), bf16[4,2,64,512]{3,1,2,0:T(2,128)(2,1)}, u32[]{:S(2)}, u32[]{:S(2)}) async-start(bf16[4,2,64,512]{3,1,2,0:T(2,128)(2,1)} %copy.184), calls=%async_computation.8 | async-start | bytes 1048576 | tf_op jit(solution)/shard_map/all_to_all | solution.py:252
  495.0 11.1 %copy-start.8 = (bf16[8,128,1024]{2,1,0:T(8,128)(2,1)S(1)}, bf16[8,128,1024]{2,1,0:T(8,128)(2,1)}, u32[]{:S(2)}) copy-start(bf16[8,128,1024]{2,1,0:T(8,128)(2,1)} %copy.154) | copy-start | bytes 6291460
  501.9 13.0 %all-to-all-start.10 = ((bf16[4,2,64,512]{3,1,2,0:T(2,128)(2,1)}), bf16[4,2,64,512]{3,1,2,0:T(2,128)(2,1)}, u32[]{:S(2)}, u32[]{:S(2)}) async-start(bf16[4,2,64,512]{3,1,2,0:T(2,128)(2,1)} %copy.190), calls=%async_computation.10 | async-start | bytes 1048576 | tf_op jit(solution)/shard_map/all_to_all | solution.py:259
  511.9 6.6 %copy-start.6 = (bf16[8,128,1024]{2,1,0:T(8,128)(2,1)S(1)}, bf16[8,128,1024]{2,1,0:T(8,128)(2,1)}, u32[]{:S(2)}) copy-start(bf16[8,128,1024]{2,1,0:T(8,128)(2,1)} %copy.171) | copy-start | bytes 6291460
  514.9 18.0 %all-to-all-start.11 = ((bf16[4,2,64,1024]{3,1,2,0:T(2,128)(2,1)}), bf16[4,2,64,1024]{3,1,2,0:T(2,128)(2,1)S(1)}, u32[]{:S(2)}, u32[]{:S(2)}) async-start(bf16[4,2,64,1024]{3,1,2,0:T(2,128)(2,1)} %copy.195), calls=%async_computation.11 | async-start | bytes 2097152 | tf_op jit(solution)/shard_map/all_to_all | solution.py:266
  532.9 19.0 %all-to-all-start.7 = ((bf16[4,2,64,1024]{3,1,2,0:T(2,128)(2,1)}), bf16[4,2,64,1024]{3,1,2,0:T(2,128)(2,1)}, u32[]{:S(2)}, u32[]{:S(2)}) async-start(bf16[4,2,64,1024]{3,1,2,0:T(2,128)(2,1)} %copy.173), calls=%async_computation.7 | async-start | bytes 2097152 | tf_op jit(solution)/shard_map/all_to_all | solution.py:245
  551.9 6.8 %copy-start.1 = (f32[8,64,1024]{2,1,0:T(8,128)S(1)}, f32[8,64,1024]{2,1,0:T(8,128)}, u32[]{:S(2)}) copy-start(f32[8,64,1024]{2,1,0:T(8,128)} %param.31) | copy-start | bytes 6291460
Sparse Core Ops, SparseCore 0:
  128.0 61.6 all-gather.4
  200.1 61.4 all-gather.6
  281.9 73.5 all-reduce.6
  411.3 71.1 all-reduce.8
